TPU v7x, 32 devices: a whole 2x2x4 slice. The times are simulated.
32 devices in a mesh: seq: 8 (over y, x, core), tp: 4 (over z).
Axes of the slice: x: 2, y: 2, z: 4, core: 2. Of those that a mesh axis runs over, the one named last changes fastest.
Arguments:
- semantic_states: bfloat16 [2048, 3584], P('seq', 'tp'), may hold values from -6 to 6
- token_projection: bfloat16 [3584, 1024], P('tp'), may hold values from -0.09375 to 0.09375
- phase_offsets: float32 [4, 1024], replicated, may hold values from -6 to 6
- target_spectrum: float32 [8192, 80], P(('seq', 'tp')), may hold values from -6 to 6
- noise: float32 [8192, 80], P(('seq', 'tp')), may hold values from -6 to 6
- timestep: float32 [1], replicated, may hold values from 0.05 to 0.95
- frame_lift: bfloat16 [80, 1024], replicated, may hold values from -0.625 to 0.625
- time_weight: float32 [256, 2048], replicated, may hold values from -0.375 to 0.375
- attention_weight: bfloat16 [1024, 3, 1024], P(None, None, 'tp'), may hold values from -2 to 2
- head_mixing: bfloat16 [1024, 1024], P('tp'), may hold values from -0.1875 to 0.1875
- velocity_head: bfloat16 [1024, 80], replicated, may hold values from -0.1875 to 0.1875
- group_index: int32 [8192], replicated, may hold values from 0 to 127, never falling along the last dimension, each value on 1 to 128 neighbouring positions
- block_order: int32 [16], replicated, may hold values from 0 to 15, each once
Outputs:
- velocity: float32 [8192, 80], P(('seq', 'tp'))
Inputs may be any that keep to these rules, and one draw needn't show every extreme that they name: `group_index`: Non-decreasing along the natural frame position; every group 0 to 127 holds 1 to 128 consecutive frames, one exactly 128. A permutation: stored block b holds the frames of natural block block_order[b] and the tokens of those frames.
All inputs are finite; a program needn't handle non-finite values.
Results may differ from a plain program's by a relative error of at most 0.006.
Values may be sent and summed in bfloat16 or wider, within the bound.
A program may use at most 64 MiB of HBM per device.

v0:
```python
import math

import jax
import jax.numpy as jnp
from jax import lax
from jax.sharding import PartitionSpec as P

HEADS = 16


masked_score = -1e30


def layer_norm(values):
    center = values - jnp.mean(values, axis=-1, keepdims=True)
    spread = jnp.mean(center * center, axis=-1, keepdims=True)
    return center * lax.rsqrt(spread + 1e-06)


def time_modulation(timestep, time_weight):
    half_count = time_weight.shape[0] // 2
    rates = jnp.exp(-math.log(10000.0) * jnp.arange(half_count, dtype=jnp.float32) / half_count)
    angles = 1000.0 * timestep[0] * rates
    features = jnp.concatenate([jnp.cos(angles), jnp.sin(angles)])
    return jnp.dot(jax.nn.silu(features)[None, :], time_weight, precision=lax.Precision.HIGHEST)[0]


def body(
    semantic_states,
    token_projection,
    phase_offsets,
    target_spectrum,
    noise,
    timestep,
    frame_lift,
    time_weight,
    attention_weight,
    head_mixing,
    velocity_head,
    group_index,
    block_order,
):
    width = token_projection.shape[1]
    frame_count = target_spectrum.shape[0]
    upsample = phase_offsets.shape[0]
    tp_count = lax.axis_size("tp")
    head_cols = attention_weight.shape[2]
    head_dim = width // HEADS
    local_heads = head_cols // head_dim
    frames_dev = frame_count * tp_count
    block_len = frames_dev // 2
    seq_index = lax.axis_index("seq")
    picked = semantic_states
    cond = lax.psum_scatter(
        jnp.dot(picked, token_projection, preferred_element_type=jnp.float32),
        "tp",
        scatter_dimension=0,
        tiled=True,
    )
    moment = timestep[0]
    mixed = ((1.0 - moment) * noise + moment * target_spectrum).astype(jnp.bfloat16)
    lifted = jnp.dot(mixed, frame_lift, preferred_element_type=jnp.float32)
    start_state = (
        lifted.reshape(frame_count // upsample, upsample, width)
        + cond[:, None, :]
        + phase_offsets[None]
    ).reshape(frame_count, width)
    modulation = time_modulation(timestep, time_weight)
    normed = (layer_norm(start_state) * (1.0 + modulation[width:]) + modulation[:width]).astype(
        jnp.bfloat16
    )
    attention_local = attention_weight.reshape(width, 3 * head_cols)
    projected = jnp.dot(
        lax.all_gather(normed, "tp", axis=0, tiled=True),
        attention_local,
        preferred_element_type=jnp.float32,
    ).astype(jnp.bfloat16)
    queries = projected[:, :head_cols].reshape(frames_dev, local_heads, head_dim)
    keys = projected[:, head_cols : 2 * head_cols]
    values = projected[:, 2 * head_cols :]

    def block_groups(stored):
        natural = lax.dynamic_index_in_dim(block_order, stored, 0, keepdims=False)
        return lax.dynamic_slice_in_dim(group_index, natural * block_len, block_len)

    def shard_groups(shard):
        return jnp.concatenate([block_groups(2 * shard), block_groups(2 * shard + 1)])

    query_groups = shard_groups(seq_index)
    factor = 1.0 / math.sqrt(head_dim)

    def attend_shard(carry, key_shard, value_shard, key_groups):
        highest, denominator, accum = carry
        key_heads = key_shard.reshape(frames_dev, local_heads, head_dim)
        value_heads = value_shard.reshape(frames_dev, local_heads, head_dim)
        scores = (
            jnp.einsum("qhd,khd->hqk", queries, key_heads, preferred_element_type=jnp.float32)
            * factor
        )
        allowed = (key_groups[None, :] <= query_groups[:, None])[None]
        new_high = jnp.maximum(highest, jnp.max(jnp.where(allowed, scores, masked_score), axis=2))
        expo = jnp.where(allowed, jnp.exp(scores - new_high[:, :, None]), 0.0)
        shrink = jnp.exp(highest - new_high)
        denominator = denominator * shrink + jnp.sum(expo, axis=2)
        accum = accum * shrink[:, :, None] + jnp.einsum(
            "hqk,khd->hqd",
            expo.astype(jnp.bfloat16),
            value_heads,
            preferred_element_type=jnp.float32,
        )
        return (new_high, denominator, accum)

    def visit(carry, key_shard, value_shard, shard):
        key_groups = shard_groups(shard)
        return attend_shard(carry, key_shard, value_shard, key_groups)

    initial = (
        jnp.full((local_heads, frames_dev), masked_score, jnp.float32),
        jnp.zeros((local_heads, frames_dev), jnp.float32),
        jnp.zeros((local_heads, frames_dev, head_dim), jnp.float32),
    )
    key_piece = lax.all_gather(keys, "seq", axis=0, tiled=True)
    value_piece = lax.all_gather(values, "seq", axis=0, tiled=True)
    shard_count = key_piece.shape[0] // frames_dev

    def advance(state, item):
        key_shard, value_shard, offset = item
        return (visit(state, key_shard, value_shard, offset), None)

    items = (
        key_piece.reshape(shard_count, frames_dev, head_cols),
        value_piece.reshape(shard_count, frames_dev, head_cols),
        jnp.arange(shard_count, dtype=jnp.int32),
    )
    result, _ = lax.scan(advance, initial, items)
    highest, denominator, accum = result
    attended = (
        (accum / denominator[:, :, None])
        .transpose(1, 0, 2)
        .reshape(frames_dev, head_cols)
        .astype(jnp.bfloat16)
    )
    picked = attended
    update = lax.psum_scatter(
        jnp.dot(picked, head_mixing, preferred_element_type=jnp.float32).astype(jnp.bfloat16),
        "tp",
        scatter_dimension=0,
        tiled=True,
    ).astype(jnp.float32)
    final_state = start_state + update
    closing = layer_norm(final_state).astype(jnp.bfloat16)
    return jnp.dot(closing, velocity_head, preferred_element_type=jnp.float32)


def solution(mesh):
    in_specs = (
        P("seq", "tp"),
        P("tp", None),
        P(),
        P(("seq", "tp"), None),
        P(("seq", "tp"), None),
        P(),
        P(),
        P(),
        P(None, None, "tp"),
        P("tp", None),
        P(),
        P(),
        P(),
    )
    out_specs = P(("seq", "tp"), None)
    return jax.shard_map(body, mesh=mesh, in_specs=in_specs, out_specs=out_specs, check_vma=False)
```

profile of v0, /device:TPU:0, one launch (start us, length us, event | category | flops | bytes accessed | tf_op | source)
XLA Modules:
  0.0 383.8 jit_solution(14537498321596712124)
XLA Ops:
  6.5 3.5 fusion.29
  14.8 25.2 %reduce-scatter.3.cloned.1.call-done = f32[64,1024]{1,0:T(8,128)} async-done(((f32[256,1024]{1,0:T(8,128)}), f32[64,1024]{1,0:T(8,128)}) %reduce-scatter.3.cloned.1.call-update) | async-done | bytes 262160 | tf_op jit(solution)/shard_map/reduce_scatter | solution.py:54
  51.3 42.1 %all-gather.4.cloned.1.call-done = bf16[1024,1024]{1,0:T(8,128)(2,1)} async-done(((bf16[256,1024]{1,0:T(8,128)(2,1)}), bf16[1024,1024]{1,0:T(8,128)(2,1)}) %all-gather.4.cloned.1.call-update) | async-done | bytes 2097168 | tf_op jit(solution)/shard_map/all_gather | solution.py:74
  93.4 3.9 %convolution_convert_fusion.1 = bf16[1024,768]{0,1:T(8,128)(2,1)S(1)} fusion(bf16[1024,1024]{1,0:T(8,128)(2,1)} %all-gather.4.cloned.1.call-done, bf16[1024,768]{0,1:T(8,128)(2,1)} %bitcast.85), kind=kOutput, calls=%fused_computation.24 | convolution fusion | flops 1611399168 | bytes 5242880 | tf_op jit(solution)/shard_map/dot_general | solution.py:73
  101.9 32.0 %all-gather.8.cloned.1.call-done = bf16[8192,256]{0,1:T(8,128)(2,1)} async-done(((bf16[1024,256]{0,1:T(8,128)(2,1)}), bf16[8192,256]{0,1:T(8,128)(2,1)}) %all-gather.8.cloned.1.call-update) | async-done | bytes 4194320 | tf_op jit(solution)/shard_map/all_gather | solution.py:123
  134.0 4.8 %copy.26 = bf16[32,8,8,1024]{3,2,0,1:T(8,128)(2,1)} copy(bf16[32,8,8,1024]{3,2,1,0:T(8,128)(2,1)} %bitcast.82) | data formatting | bytes 8388608 | tf_op jit(solution)/shard_map/reshape | solution.py:132
  138.7 33.9 %all-gather.6.cloned.1.call-done = bf16[8192,256]{0,1:T(8,128)(2,1)} async-done(((bf16[1024,256]{0,1:T(8,128)(2,1)}), bf16[8192,256]{0,1:T(8,128)(2,1)}) %all-gather.6.cloned.1.call-update) | async-done | bytes 4194320 | tf_op jit(solution)/shard_map/all_gather | solution.py:122
  172.6 4.8 %copy.27 = bf16[32,8,8,1024]{3,2,0,1:T(8,128)(2,1)} copy(bf16[32,8,8,1024]{3,2,1,0:T(8,128)(2,1)} %bitcast.83) | data formatting | bytes 8388608 | tf_op jit(solution)/shard_map/reshape | solution.py:131
  177.4 146.6 %while.17 = (s32[]{:T(128)}, f32[4,1024]{1,0:T(4,128)S(1)}, f32[4,1024]{1,0:T(4,128)S(1)}, f32[4,1024,64]{1,2,0:T(8,128)}, s32[8]{0:T(128)S(1)}, /*index=5*/s32[...) while((s32[]{:T(128)}, f32[4,1024]{1,0:T(4,128)S(1)}, ...), condition=%wide.region_6.7_spmd.clone, body=%wide.region_3.6_spmd.clone.sunk | while | flops 1121735680 | bytes 60580252 | solution.py:135
  186.6 3.7 fusion.61
  190.2 4.6 %fusion.63 = f32[4,1024,64]{1,2,0:T(8,128)} fusion(bf16[1024,4,64]{0,2,1:T(8,128)(2,1)S(1)} %bitcast.79, f32[4,1024,1024]{2,1,0:T(8,128)S(1)} %get-tuple-element.331, f32[4,1024]{1,0:T(4,128)S(1)} %select_maximum_fusion.2, pred[1024,1024]{0,1:T(8,128)(4,1)S(1)} %broadcast_compare_fusion.2, f32[4,1024,64]{1,2,0:T(8,128)} %get-tuple-element.356, ...), kind=kOutput, calls=%fused_computation.10.clone.1 | convolution fusion | flops 554434560 | bytes 20480000 | tf_op jit(solution)/shard_map/while/body/eval_jaxpr/hqk,khd->hqd/dot_general | solution.py:105
  201.0 3.0 fusion.60
  204.0 3.7 fusion.61
  207.7 5.6 %fusion.63 = f32[4,1024,64]{1,2,0:T(8,128)} fusion(bf16[1024,4,64]{0,2,1:T(8,128)(2,1)S(1)} %bitcast.79, f32[4,1024,1024]{2,1,0:T(8,128)S(1)} %get-tuple-element.331, f32[4,1024]{1,0:T(4,128)S(1)} %select_maximum_fusion.2, pred[1024,1024]{0,1:T(8,128)(4,1)S(1)} %broadcast_compare_fusion.2, f32[4,1024,64]{1,2,0:T(8,128)} %get-tuple-element.356, ...), kind=kOutput, calls=%fused_computation.10.clone.1 | convolution fusion | flops 554434560 | bytes 20480000 | tf_op jit(solution)/shard_map/while/body/eval_jaxpr/hqk,khd->hqd/dot_general | solution.py:105
  222.4 3.7 fusion.61
  226.1 5.6 %fusion.63 = f32[4,1024,64]{1,2,0:T(8,128)} fusion(bf16[1024,4,64]{0,2,1:T(8,128)(2,1)S(1)} %bitcast.79, f32[4,1024,1024]{2,1,0:T(8,128)S(1)} %get-tuple-element.331, f32[4,1024]{1,0:T(4,128)S(1)} %select_maximum_fusion.2, pred[1024,1024]{0,1:T(8,128)(4,1)S(1)} %broadcast_compare_fusion.2, f32[4,1024,64]{1,2,0:T(8,128)} %get-tuple-element.356, ...), kind=kOutput, calls=%fused_computation.10.clone.1 | convolution fusion | flops 554434560 | bytes 20480000 | tf_op jit(solution)/shard_map/while/body/eval_jaxpr/hqk,khd->hqd/dot_general | solution.py:105
  237.9 3.0 fusion.60
  240.9 3.7 fusion.61
  244.6 5.6 %fusion.63 = f32[4,1024,64]{1,2,0:T(8,128)} fusion(bf16[1024,4,64]{0,2,1:T(8,128)(2,1)S(1)} %bitcast.79, f32[4,1024,1024]{2,1,0:T(8,128)S(1)} %get-tuple-element.331, f32[4,1024]{1,0:T(4,128)S(1)} %select_maximum_fusion.2, pred[1024,1024]{0,1:T(8,128)(4,1)S(1)} %broadcast_compare_fusion.2, f32[4,1024,64]{1,2,0:T(8,128)} %get-tuple-element.356, ...), kind=kOutput, calls=%fused_computation.10.clone.1 | convolution fusion | flops 554434560 | bytes 20480000 | tf_op jit(solution)/shard_map/while/body/eval_jaxpr/hqk,khd->hqd/dot_general | solution.py:105
  256.3 3.0 fusion.60
  259.4 3.7 fusion.61
  263.0 5.6 %fusion.63 = f32[4,1024,64]{1,2,0:T(8,128)} fusion(bf16[1024,4,64]{0,2,1:T(8,128)(2,1)S(1)} %bitcast.79, f32[4,1024,1024]{2,1,0:T(8,128)S(1)} %get-tuple-element.331, f32[4,1024]{1,0:T(4,128)S(1)} %select_maximum_fusion.2, pred[1024,1024]{0,1:T(8,128)(4,1)S(1)} %broadcast_compare_fusion.2, f32[4,1024,64]{1,2,0:T(8,128)} %get-tuple-element.356, ...), kind=kOutput, calls=%fused_computation.10.clone.1 | convolution fusion | flops 554434560 | bytes 20480000 | tf_op jit(solution)/shard_map/while/body/eval_jaxpr/hqk,khd->hqd/dot_general | solution.py:105
  274.8 3.0 fusion.60
  277.8 3.7 fusion.61
  281.5 5.6 %fusion.63 = f32[4,1024,64]{1,2,0:T(8,128)} fusion(bf16[1024,4,64]{0,2,1:T(8,128)(2,1)S(1)} %bitcast.79, f32[4,1024,1024]{2,1,0:T(8,128)S(1)} %get-tuple-element.331, f32[4,1024]{1,0:T(4,128)S(1)} %select_maximum_fusion.2, pred[1024,1024]{0,1:T(8,128)(4,1)S(1)} %broadcast_compare_fusion.2, f32[4,1024,64]{1,2,0:T(8,128)} %get-tuple-element.356, ...), kind=kOutput, calls=%fused_computation.10.clone.1 | convolution fusion | flops 554434560 | bytes 20480000 | tf_op jit(solution)/shard_map/while/body/eval_jaxpr/hqk,khd->hqd/dot_general | solution.py:105
  296.3 3.7 fusion.61
  299.9 5.6 %fusion.63 = f32[4,1024,64]{1,2,0:T(8,128)} fusion(bf16[1024,4,64]{0,2,1:T(8,128)(2,1)S(1)} %bitcast.79, f32[4,1024,1024]{2,1,0:T(8,128)S(1)} %get-tuple-element.331, f32[4,1024]{1,0:T(4,128)S(1)} %select_maximum_fusion.2, pred[1024,1024]{0,1:T(8,128)(4,1)S(1)} %broadcast_compare_fusion.2, f32[4,1024,64]{1,2,0:T(8,128)} %get-tuple-element.356, ...), kind=kOutput, calls=%fused_computation.10.clone.1 | convolution fusion | flops 554434560 | bytes 20480000 | tf_op jit(solution)/shard_map/while/body/eval_jaxpr/hqk,khd->hqd/dot_general | solution.py:105
  311.7 3.0 fusion.60
  314.7 3.7 fusion.61
  318.4 5.6 %fusion.63 = f32[4,1024,64]{1,2,0:T(8,128)} fusion(bf16[1024,4,64]{0,2,1:T(8,128)(2,1)S(1)} %bitcast.79, f32[4,1024,1024]{2,1,0:T(8,128)S(1)} %get-tuple-element.331, f32[4,1024]{1,0:T(4,128)S(1)} %select_maximum_fusion.2, pred[1024,1024]{0,1:T(8,128)(4,1)S(1)} %broadcast_compare_fusion.2, f32[4,1024,64]{1,2,0:T(8,128)} %get-tuple-element.356, ...), kind=kOutput, calls=%fused_computation.10.clone.1 | convolution fusion | flops 554434560 | bytes 20480000 | tf_op jit(solution)/shard_map/while/body/eval_jaxpr/hqk,khd->hqd/dot_general | solution.py:105
  325.4 3.2 convolution_convert_fusion
  328.6 44.0 %reduce-scatter.5.cloned.1.call-done = bf16[256,1024]{1,0:T(8,128)(2,1)} async-done(((bf16[1024,1024]{1,0:T(8,128)(2,1)}), bf16[256,1024]{1,0:T(8,128)(2,1)}) %reduce-scatter.5.cloned.1.call-update) | async-done | bytes 524304 | tf_op jit(solution)/shard_map/reduce_scatter | solution.py:144
  (131 shorter events, 66.5 us)
Async XLA Ops:
  6.5 7.2 %copy-start = (f32[256,2048]{1,0:T(8,128)S(1)}, f32[256,2048]{1,0:T(8,128)}, u32[]{:S(2)}) copy-start(f32[256,2048]{1,0:T(8,128)} %param.22) | copy-start | bytes 6291460
  6.5 4.2 %copy-start.8 = (f32[4,1024]{1,0:T(4,128)S(1)}, f32[4,1024]{1,0:T(4,128)}, u32[]{:S(2)}) copy-start(f32[4,1024]{1,0:T(4,128)} %param.17) | copy-start | bytes 49156
  6.5 33.5 %reduce-scatter.3.cloned.1.call-start = ((), (), s32[]{:S(2)}) async-start(), calls=%async_computation.2 | async-start | bytes 1310720 | tf_op jit(solution)/shard_map/reduce_scatter | solution.py:54
  10.0 83.3 %all-gather.4.cloned.1.call-start = ((), (), s32[]{:S(2)}) async-start(), calls=%async_computation.3 | async-start | bytes 2621440 | tf_op jit(solution)/shard_map/all_gather | solution.py:74
  10.8 34.1 %copy-start.3 = (bf16[80,1024]{1,0:T(8,128)(2,1)S(1)}, bf16[80,1024]{1,0:T(8,128)(2,1)}, u32[]{:S(2)}) copy-start(bf16[80,1024]{1,0:T(8,128)(2,1)} %param.21) | copy-start | bytes 491524
  10.8 34.1 %copy-start.5 = (f32[256,80]{0,1:T(8,128)S(1)}, f32[256,80]{0,1:T(8,128)}, u32[]{:S(2)}) copy-start(f32[256,80]{0,1:T(8,128)} %param.18) | copy-start | bytes 245764
  10.8 34.1 %copy-start.6 = (f32[256,80]{0,1:T(8,128)S(1)}, f32[256,80]{0,1:T(8,128)}, u32[]{:S(2)}) copy-start(f32[256,80]{0,1:T(8,128)} %param.19) | copy-start | bytes 245764
  46.5 1.1 copy-start.1
  48.6 85.3 %all-gather.8.cloned.1.call-start = ((), (), s32[]{:S(2)}) async-start(), calls=%async_computation.5 | async-start | bytes 4718592 | tf_op jit(solution)/shard_map/all_gather | solution.py:123
  97.2 1.9 copy-start.7
  98.4 74.3 %all-gather.6.cloned.1.call-start = ((), (), s32[]{:S(2)}) async-start(), calls=%async_computation.4 | async-start | bytes 4718592 | tf_op jit(solution)/shard_map/all_gather | solution.py:122
  98.9 273.7 %reduce-scatter.5.cloned.1.call-start = ((), (), s32[]{:S(2)}) async-start(), calls=%async_computation.6 | async-start | bytes 2621440 | tf_op jit(solution)/shard_map/reduce_scatter | solution.py:144
  324.0 48.6 %copy-start.2 = (f32[256,1024]{1,0:T(8,128)S(1)}, f32[256,1024]{1,0:T(8,128)}, u32[]{:S(2)}) copy-start(f32[256,1024]{1,0:T(8,128)} %copy-done.1) | copy-start | bytes 3145732
  325.4 49.8 %copy-start.4 = (bf16[1024,80]{0,1:T(8,128)(2,1)S(1)}, bf16[1024,80]{0,1:T(8,128)(2,1)}, u32[]{:S(2)}) copy-start(bf16[1024,80]{0,1:T(8,128)(2,1)} %param.25) | copy-start | bytes 491524
Sparse Core Ops, SparseCore 0:
  10.2 29.8 reduce-scatter.2
  48.7 44.5 all-gather.3
  98.5 35.4 all-gather.7
  135.9 36.7 all-gather.5
  328.7 43.8 reduce-scatter.4
where the time goes:
time: 385 us; the launch traced here: 384 us
  waiting for transfers between devices  178 us (46%)
  matrix products  83.4 us (22%)
  local copies, waits for them, and re-layouts  50.3 us (13%)
  other arithmetic  40.2 us (10%)
  loops' own time  16.5 us (4%)
  between operations  15.2 us (4%)
    reduce_scatter x1, waiting for transfers between devices, body(): lax.psum_scatter(jnp.dot(picked, head_mixing, preferred_element_type=jnp....  44 us
    dot_general x8, matrix products, attend_shard(): jnp.einsum('hqk,khd->hqd', expo.astype(jnp.bfloat16), value_heads, prefer...  43.9 us
    all_gather x1, waiting for transfers between devices, body(): lax.all_gather(normed, 'tp', axis=0, tiled=True)  42.1 us
    all_gather x1, waiting for transfers between devices, body(): key_piece = lax.all_gather(keys, 'seq', axis=0, tiled=True)  33.9 us
    all_gather x1, waiting for transfers between devices, body(): value_piece = lax.all_gather(values, 'seq', axis=0, tiled=True)  32 us
    reduce_sum x8, other arithmetic, attend_shard(): denominator = denominator * shrink + jnp.sum(expo, axis=2)  29.3 us
    reduce_scatter x1, waiting for transfers between devices, body(): lax.psum_scatter(jnp.dot(picked, token_projection, preferred_element_type...  25.2 us
    dot_general x8, matrix products, attend_shard(): jnp.einsum('qhd,khd->hqk', queries, key_heads, preferred_element_type=jnp...  24.2 us
  transfers between devices with their start and end apart: 5, of which 5 were waited for; matrix products, arithmetic and copies ran while one was open for 3% of the time, Pallas kernels for 0%

commit v1 on v0

v1 whole, which is shorter than its diff:
```python
import functools
import math

import jax
import jax.numpy as jnp
from jax import lax
from jax.experimental import pallas as pl
from jax.experimental.pallas import tpu as pltpu
from jax.sharding import PartitionSpec as P

HEADS = 16
MESH = pl.DeviceIdType.MESH
masked_score = -1e30


def layer_norm(values):
    center = values - jnp.mean(values, axis=-1, keepdims=True)
    spread = jnp.mean(center * center, axis=-1, keepdims=True)
    return center * lax.rsqrt(spread + 1e-06)


def time_modulation(timestep, time_weight):
    half_count = time_weight.shape[0] // 2
    rates = jnp.exp(-math.log(10000.0) * jnp.arange(half_count, dtype=jnp.float32) / half_count)
    angles = 1000.0 * timestep[0] * rates
    features = jnp.concatenate([jnp.cos(angles), jnp.sin(angles)])
    return jnp.dot(jax.nn.silu(features)[None, :], time_weight, precision=lax.Precision.HIGHEST)[0]


def project_kernel(
    dims,
    states_ref,
    proj_ref,
    mixed_ref,
    lift_ref,
    phase_ref,
    mod_ref,
    weight_ref,
    start_ref,
    kv_all,
    q_all,
    part_buf,
    got_buf,
    cond_buf,
    mix_buf,
    kv_buf,
    q_buf,
    part_send,
    part_recv,
    cond_send,
    cond_recv,
    mix_send,
    mix_recv,
    kv_send,
    kv_recv,
    q_send,
    q_recv,
):
    seq_n, tp_n, heads, ranks, dim, upsample = dims
    me = lax.axis_index("seq")
    tp = lax.axis_index("tp")
    tokens = cond_buf.shape[1]
    frames = mixed_ref.shape[0]
    cols = heads * dim

    barrier = pltpu.get_barrier_semaphore()
    for d in range(1, tp_n):
        pl.semaphore_signal(
            barrier, inc=1, device_id=(me, lax.rem(tp + d, tp_n)), device_id_type=MESH
        )
    for d in range(1, seq_n):
        pl.semaphore_signal(
            barrier, inc=1, device_id=(lax.rem(me + d, seq_n), tp), device_id_type=MESH
        )
    pl.semaphore_wait(barrier, tp_n - 1 + seq_n - 1)

    def tp_copy(src, dst, send, recv, d):
        return pltpu.make_async_remote_copy(
            src_ref=src,
            dst_ref=dst,
            send_sem=send.at[d],
            recv_sem=recv.at[d],
            device_id=(me, lax.rem(tp + d, tp_n)),
            device_id_type=MESH,
        )

    def mix_copy(d):
        return tp_copy(mixed_ref, mix_buf.at[d], mix_send, mix_recv, d)

    def part_copy(d):
        return tp_copy(part_buf.at[d], got_buf.at[d], part_send, part_recv, d)

    def cond_copy(d):
        return tp_copy(cond_buf.at[0], cond_buf.at[d], cond_send, cond_recv, d)

    for d in range(1, tp_n):
        mix_copy(d).start()
    mix_buf[0] = mixed_ref[...]
    own = None
    for d in list(range(1, tp_n)) + [0]:
        rows = pl.ds(pl.multiple_of(lax.rem(tp + d, tp_n) * tokens, tokens), tokens)
        piece = jnp.dot(states_ref[rows, :], proj_ref[...], preferred_element_type=jnp.float32)
        if d:
            part_buf[d] = piece.astype(jnp.bfloat16)
            part_copy(d).start()
        else:
            own = piece
    for d in range(1, tp_n):
        part_copy(d).wait_recv()
        own = own + got_buf[d].astype(jnp.float32)
    cond_buf[0] = own.astype(jnp.bfloat16)
    for d in range(1, tp_n):
        cond_copy(d).start()

    frame_at = lax.broadcasted_iota(jnp.int32, (frames, tokens), 0)
    first = lax.broadcasted_iota(jnp.int32, (frames, tokens), 1) * upsample
    spread = jnp.where((frame_at >= first) & (frame_at < first + upsample), 1.0, 0.0).astype(
        jnp.bfloat16
    )
    q_factor = math.log2(math.e) / math.sqrt(dim)

    def kv_copy(chunk, d):
        dest = lax.rem(me + d, seq_n)
        return pltpu.make_async_remote_copy(
            src_ref=kv_buf.at[chunk, dest // ranks],
            dst_ref=kv_all.at[me, chunk],
            send_sem=kv_send.at[d, chunk],
            recv_sem=kv_recv.at[d, chunk],
            device_id=(dest, tp),
            device_id_type=MESH,
        )

    def q_copy(chunk, d):
        dest = lax.rem(me + d, seq_n)
        return pltpu.make_async_remote_copy(
            src_ref=q_buf.at[chunk, dest // ranks],
            dst_ref=q_all.at[me, chunk // ranks],
            send_sem=q_send.at[d, chunk // ranks],
            recv_sem=q_recv.at[d, chunk // ranks],
            device_id=(dest, tp),
            device_id_type=MESH,
        )

    def own_kv(chunk):
        return pltpu.make_async_copy(
            kv_buf.at[chunk, me // ranks], kv_all.at[me, chunk], kv_send.at[0, chunk]
        )

    def own_q(chunk):
        return pltpu.make_async_copy(
            q_buf.at[chunk, me // ranks],
            q_all.at[me, chunk // ranks],
            q_send.at[0, chunk // ranks],
        )

    @pl.loop(0, tp_n)
    def _(step):
        chunk = lax.rem(tp - step + tp_n, tp_n)

        @pl.when(step > 0)
        def _():
            mix_copy(step).wait_recv()
            cond_copy(step).wait_recv()

        state = jnp.dot(mix_buf[step], lift_ref[...], preferred_element_type=jnp.float32)
        state = state + jnp.dot(spread, cond_buf[step], preferred_element_type=jnp.float32)
        state = (
            state.reshape(frames // 8, 8, state.shape[1]) + phase_ref[...][None]
        ).reshape(state.shape)

        @pl.when(step == 0)
        def _():
            start_ref[...] = state

        normed = (layer_norm(state) * mod_ref[1:2, :] + mod_ref[0:1, :]).astype(jnp.bfloat16)
        for kind in range(3):
            made = jnp.dot(
                normed,
                weight_ref[:, kind * cols : (kind + 1) * cols],
                preferred_element_type=jnp.float32,
            ).T
            if kind == 0:
                q_buf[chunk] = (made * q_factor).astype(jnp.bfloat16).reshape(heads, dim, frames)
            else:
                kv_buf[chunk, :, (kind - 1) * dim : kind * dim, :] = made.astype(
                    jnp.bfloat16
                ).reshape(heads, dim, frames)
        for d in range(1, seq_n):
            kv_copy(chunk, d).start()

            @pl.when(lax.rem(chunk, ranks) == lax.rem(lax.rem(me + d, seq_n), ranks))
            def _():
                q_copy(chunk, d).start()

        own_kv(chunk).start()

        @pl.when(lax.rem(chunk, ranks) == lax.rem(me, ranks))
        def _():
            own_q(chunk).start()

    for d in range(1, tp_n):
        mix_copy(d).wait_send()
        part_copy(d).wait_send()
        cond_copy(d).wait_send()
    for chunk in range(tp_n):
        own_kv(chunk).wait()
        for d in range(1, seq_n):
            kv_copy(chunk, d).wait()
    for k in range(tp_n // ranks):
        own_q(k * ranks).wait()
        for d in range(1, seq_n):
            q_copy(k * ranks, d).wait()


def attend_kernel(
    dims,
    natural_ref,
    place_ref,
    first_ref,
    ends_ref,
    q_ref,
    kv_ref,
    out_ref,
    key_buf,
    value_buf,
):
    seq_n, tp_n, dim, block_len = dims
    frames = q_ref.shape[-1]
    per_block = block_len // frames
    block_count = place_ref.shape[0]
    tile = pl.program_id(0)
    value_rows = value_buf.shape[1]

    @pl.when(tile == 0)
    def _():
        @pl.loop(0, seq_n * tp_n)
        def _(i):
            at = pl.ds(pl.multiple_of(i * frames, frames), frames)
            key_buf[at, :] = kv_ref[i, :dim, :].astype(jnp.float32).T.astype(jnp.bfloat16)
            value_buf[i, :dim, :] = kv_ref[i, dim:, :]
            value_buf[i, dim:, :] = jnp.ones((value_rows - dim, frames), jnp.bfloat16)

    queries = q_ref[0]
    natural = natural_ref[tile]
    base = natural * block_len
    at = first_ref[tile] + lax.broadcasted_iota(jnp.int32, (1, frames), 1)
    ends = ends_ref[...]
    stop = jnp.min(jnp.where(ends > at, ends, 1 << 30), axis=0, keepdims=True)

    def visit(carry, stored, count, limit):
        highest, total = carry
        keys = key_buf[pl.ds(pl.multiple_of(stored * block_len, block_len), count), :]
        scores = jnp.dot(keys, queries, preferred_element_type=jnp.float32)
        if limit is not None:
            row = lax.broadcasted_iota(jnp.int32, (count, frames), 0)
            scores = jnp.where(row < limit, scores, masked_score)
        above = jnp.maximum(highest, jnp.max(scores, axis=0, keepdims=True))
        expo = jnp.exp2(scores - above).astype(jnp.bfloat16)
        total = total * jnp.exp2(highest - above)
        for c in range(pl.cdiv(count, frames)):
            size = min(frames, count - c * frames)
            total = total + jnp.dot(
                value_buf[stored * per_block + c, :, :size],
                expo[c * frames : c * frames + size],
                preferred_element_type=jnp.float32,
            )
        return above, total

    carry = (
        jnp.full((1, frames), masked_score, jnp.float32),
        jnp.zeros((value_rows, frames), jnp.float32),
    )
    carry = visit(carry, place_ref[natural], block_len, stop - base)
    beyond = jnp.minimum(natural + 1, block_count - 1)
    carry = visit(
        carry,
        place_ref[beyond],
        128,
        jnp.where(natural + 1 < block_count, stop - base - block_len, 0),
    )

    def pair(i, carry):
        carry = visit(carry, place_ref[2 * i], block_len, None)
        return visit(carry, place_ref[2 * i + 1], block_len, None)

    carry = lax.fori_loop(0, natural // 2, pair, carry)
    carry = lax.fori_loop(
        2 * (natural // 2),
        natural,
        lambda j, carry: visit(carry, place_ref[j], block_len, None),
        carry,
    )
    total = carry[1]
    out_ref[0] = (total[:dim] / total[dim : dim + 1]).astype(jnp.bfloat16)


def return_kernel(dims, att_ref, out_ref, send_sem, recv_sem):
    seq_n, tp_n, heads, ranks = dims
    me = lax.axis_index("seq")
    tp = lax.axis_index("tp")
    rank = lax.rem(me, ranks)
    per = tp_n // ranks

    barrier = pltpu.get_barrier_semaphore()

    for p in range(heads):
        for t in range(tp_n):
            other = p * ranks + lax.rem(tp, ranks)

            @pl.when((other != me) | (t != tp))
            def _():
                pl.semaphore_signal(barrier, inc=1, device_id=(other, t), device_id_type=MESH)

    pl.semaphore_wait(barrier, seq_n * per - jnp.where(lax.rem(tp, ranks) == rank, 1, 0))

    mine = tp * heads + me // ranks

    def copy(i, k):
        s = lax.rem(me + i, seq_n)
        return pltpu.make_async_remote_copy(
            src_ref=att_ref.at[s, k],
            dst_ref=out_ref.at[mine],
            send_sem=send_sem.at[i, k],
            recv_sem=recv_sem.at[mine],
            device_id=(s, k * ranks + rank),
            device_id_type=MESH,
        )

    def local(k):
        return pltpu.make_async_copy(att_ref.at[me, k], out_ref.at[mine], send_sem.at[0, k])

    for i in range(seq_n):
        for k in range(per):
            if i:
                copy(i, k).start()
            else:

                @pl.when(k * ranks + rank != tp)
                def _():
                    copy(0, k).start()

                @pl.when(k * ranks + rank == tp)
                def _():
                    local(k).start()

    for i in range(seq_n):
        for k in range(per):
            if i:
                copy(i, k).wait_send()
            else:

                @pl.when(k * ranks + rank != tp)
                def _():
                    copy(0, k).wait_send()

                @pl.when(k * ranks + rank == tp)
                def _():
                    local(k).wait()

    for t in range(tp_n):
        for p in range(heads):
            source = p * ranks + lax.rem(tp, ranks)

            @pl.when((source != me) | (t != tp))
            def _():
                pltpu.make_async_remote_copy(
                    src_ref=att_ref.at[0, 0],
                    dst_ref=out_ref.at[t * heads + p],
                    send_sem=send_sem.at[0, 0],
                    recv_sem=recv_sem.at[t * heads + p],
                    device_id=(source, t),
                    device_id_type=MESH,
                ).wait_recv()


def body(
    semantic_states,
    token_projection,
    phase_offsets,
    target_spectrum,
    noise,
    timestep,
    frame_lift,
    time_weight,
    attention_weight,
    head_mixing,
    velocity_head,
    group_index,
    block_order,
):
    width = token_projection.shape[1]
    frame_count, bins = target_spectrum.shape
    upsample = phase_offsets.shape[0]
    tp_n = lax.axis_size("tp")
    seq_n = lax.axis_size("seq")
    cols = attention_weight.shape[2]
    dim = width // HEADS
    heads = cols // dim
    ranks = seq_n // heads
    per = tp_n // ranks
    tokens = semantic_states.shape[0] // tp_n
    frames_total = group_index.shape[0]
    block_count = block_order.shape[0]
    block_len = frames_total // block_count
    frames_dev = frame_count * tp_n
    blocks_dev = frames_dev // block_len
    me = lax.axis_index("seq")

    moment = timestep[0]
    mixed = ((1.0 - moment) * noise + moment * target_spectrum).astype(jnp.bfloat16)
    padding = -bins % 128
    mixed = jnp.pad(mixed, ((0, 0), (0, padding)))
    lift = jnp.pad(frame_lift, ((0, padding), (0, 0)))
    modulation = time_modulation(timestep, time_weight)
    mod = jnp.stack([modulation[:width], 1.0 + modulation[width:]])
    phase = jnp.tile(phase_offsets, (8 // upsample, 1))
    mixing = lax.all_gather(head_mixing, "tp", axis=0, tiled=True)

    vmem = pl.BlockSpec(memory_space=pltpu.VMEM)
    hbm = pl.BlockSpec(memory_space=pl.ANY)
    dma = pltpu.SemaphoreType.DMA
    bf16 = jnp.bfloat16
    start_state, kv_all, q_all = pl.pallas_call(
        functools.partial(project_kernel, (seq_n, tp_n, heads, ranks, dim, upsample)),
        out_shape=(
            jax.ShapeDtypeStruct((frame_count, width), jnp.float32),
            jax.ShapeDtypeStruct((seq_n, tp_n, 2 * dim, frame_count), bf16),
            jax.ShapeDtypeStruct((seq_n, per, dim, frame_count), bf16),
        ),
        in_specs=[vmem] * 7,
        out_specs=(vmem, hbm, hbm),
        scratch_shapes=[
            pltpu.VMEM((tp_n, tokens, width), bf16),
            pltpu.VMEM((tp_n, tokens, width), bf16),
            pltpu.VMEM((tp_n, tokens, width), bf16),
            pltpu.VMEM((tp_n, frame_count, bins + padding), bf16),
            pltpu.VMEM((tp_n, heads, 2 * dim, frame_count), bf16),
            pltpu.VMEM((tp_n, heads, dim, frame_count), bf16),
        ]
        + [dma((tp_n,))] * 6
        + [dma((seq_n, tp_n))] * 2
        + [dma((seq_n, per))] * 2,
        compiler_params=pltpu.CompilerParams(
            collective_id=0, has_side_effects=True, vmem_limit_bytes=40 << 20
        ),
        name="project",
    )(
        semantic_states,
        token_projection,
        mixed,
        lift,
        phase,
        mod,
        attention_weight.reshape(width, 3 * cols),
    )

    group_ids = jnp.arange(frames_total // 64, dtype=jnp.int32)
    ends = jnp.sum((group_index[None, :] <= group_ids[:, None]).astype(jnp.int32), axis=1)[:, None]
    blocks = jnp.arange(block_count, dtype=jnp.int32)
    place = jnp.sum(
        jnp.where(block_order[None, :] == blocks[:, None], blocks[None, :], 0), axis=1
    ).astype(jnp.int32)
    owner = jnp.arange(per, dtype=jnp.int32) * ranks + me % ranks
    stored = (
        jnp.arange(seq_n, dtype=jnp.int32)[:, None] * blocks_dev
        + (owner * frame_count // block_len)[None, :]
    ).reshape(-1)
    natural = jnp.sum(
        jnp.where(stored[:, None] == blocks[None, :], block_order[None, :], 0), axis=1
    ).astype(jnp.int32)
    first = natural * block_len + jnp.tile(owner * frame_count % block_len, seq_n)

    tiles = seq_n * per
    attended = pl.pallas_call(
        functools.partial(attend_kernel, (seq_n, tp_n, dim, block_len)),
        out_shape=jax.ShapeDtypeStruct((tiles, dim, frame_count), bf16),
        grid_spec=pltpu.PrefetchScalarGridSpec(
            num_scalar_prefetch=3,
            grid=(tiles,),
            in_specs=[
                vmem,
                pl.BlockSpec((1, dim, frame_count), lambda i, *_: (i, 0, 0)),
                vmem,
            ],
            out_specs=pl.BlockSpec((1, dim, frame_count), lambda i, *_: (i, 0, 0)),
            scratch_shapes=[
                pltpu.VMEM((frames_total, dim), bf16),
                pltpu.VMEM((seq_n * tp_n, dim + 16, frame_count), bf16),
            ],
        ),
        compiler_params=pltpu.CompilerParams(vmem_limit_bytes=40 << 20),
        name="attend",
    )(
        natural,
        place,
        first,
        ends,
        q_all.reshape(tiles, dim, frame_count),
        kv_all.reshape(seq_n * tp_n, 2 * dim, frame_count),
    )

    gathered = pl.pallas_call(
        functools.partial(return_kernel, (seq_n, tp_n, heads, ranks)),
        out_shape=jax.ShapeDtypeStruct((HEADS, dim, frame_count), bf16),
        in_specs=[hbm],
        out_specs=hbm,
        scratch_shapes=[dma((seq_n, per)), dma((HEADS,))],
        compiler_params=pltpu.CompilerParams(collective_id=1, has_side_effects=True),
        name="give_back",
    )(attended.reshape(seq_n, per, dim, frame_count))

    update = lax.dot_general(
        gathered.reshape(width, frame_count),
        mixing,
        (((0,), (0,)), ((), ())),
        preferred_element_type=jnp.float32,
    )
    closing = layer_norm(start_state + update).astype(jnp.bfloat16)
    return jnp.dot(closing, velocity_head, preferred_element_type=jnp.float32)


def solution(mesh):
    in_specs = (
        P("seq", "tp"),
        P("tp", None),
        P(),
        P(("seq", "tp"), None),
        P(("seq", "tp"), None),
        P(),
        P(),
        P(),
        P(None, None, "tp"),
        P("tp", None),
        P(),
        P(),
        P(),
    )
    out_specs = P(("seq", "tp"), None)
    return jax.shard_map(body, mesh=mesh, in_specs=in_specs, out_specs=out_specs, check_vma=False)
```

time: 385 us -> 203 us (0.53)
  waiting for transfers between devices: 178 us -> 0.73 us
  Pallas kernels: 0 us -> 167 us
  matrix products: 83.4 us -> 4.72 us
  other arithmetic: 40.2 us -> 1.14 us
  local copies, waits for them, and re-layouts: 50.3 us -> 14.2 us
  loops' own time: 16.5 us -> 0 us
    pallas_call x0 -> x3, Pallas kernels: none -> 167 us  [the longest x1 74.6 us: body(): pl.pallas_call(functools.partial(project_kernel, (seq_n, tp_n, heads, ran...]
    all_gather x3 -> x1, waiting for transfers between devices: 108 us -> 0.02 us  [body(): mixing = lax.all_gather(head_mixing, 'tp', axis=0, tiled=True)]
    dot_general x20 -> x1, matrix products: 80.3 us -> 2.62 us  [body(): lax.dot_general(gathered.reshape(width, frame_count), mixing, (((0,), (0,...]
    reduce_scatter x2 -> x0, waiting for transfers between devices: 69.2 us -> none  [the longest x1 44 us: body(): lax.psum_scatter(jnp.dot(picked, head_mixing, preferred_element_type=jnp....]
    reduce_sum x9 -> x2, other arithmetic: 30.5 us -> 0.67 us  [the longest x1 0.49 us: body(): jnp.sum((group_index[None, :] <= group_ids[:, None]).astype(jnp.int32), a...]
    dynamic_slice x34 -> x0, local copies, waits for them, and re-layouts: 28.5 us -> none  [the longest x16 15.5 us: body(): result, _ = lax.scan(advance, initial, items)]
    another operation x1 -> x0, loops' own time: 16.5 us -> none  [body(): result, _ = lax.scan(advance, initial, items)]
    add x4 -> x1, local copies, waits for them, and re-layouts: 7.65 us -> 0.08 us  [body(): jnp.arange(seq_n, dtype=jnp.int32)[:, None] * blocks_dev]
  transfers between devices with their start and end apart: 5 -> 1, of which waited for: 5 -> 0; matrix products, arithmetic and copies ran while one was open for 3% -> 6% of each run, Pallas kernels for 0% -> 83%
where the time goes in v1:
time: 203 us; the launch traced here: 202 us
  Pallas kernels  167 us (82%)
  local copies, waits for them, and re-layouts  14.2 us (7%)
  between operations  14.2 us (7%)
  matrix products  4.72 us (2%)
    pallas_call x1, Pallas kernels, body(): pl.pallas_call(functools.partial(project_kernel, (seq_n, tp_n, heads, ran...  74.6 us
    pallas_call x1, Pallas kernels, body(): pl.pallas_call(functools.partial(attend_kernel, (seq_n, tp_n, dim, block_...  70.7 us
    pallas_call x1, Pallas kernels, body(): pl.pallas_call(functools.partial(return_kernel, (seq_n, tp_n, heads, rank...  21.8 us
    unnamed x21, local copies, waits for them, and re-layouts  9.04 us
  transfers between devices with their start and end apart: 1, of which 0 were waited for; matrix products, arithmetic and copies ran while one was open for 6% of the time, Pallas kernels for 83%

profile of v1, /device:TPU:0, one launch (start us, length us, event | category | flops | bytes accessed | tf_op | source)
XLA Modules:
  0.0 202.1 jit_solution(14528711497504747497)
XLA Ops:
  6.5 0.0 copy-start
  6.5 0.0 all-gather.2.cloned.1.call-start
  6.5 0.7 all-gather.2.cloned.1.call-update
  7.3 1.0 copy.30
  8.2 1.0 copy.29
  9.9 0.9 pad.9.lift_ref
  10.9 0.7 tile.8
  11.6 0.6 tile.9.phase_ref
  12.2 2.6 %copy.31 = bf16[1024,3,256]{0,2,1:T(8,128)(2,1)} copy(bf16[1024,3,256]{2,0,1:T(8,128)(2,1)} %param.21) | data formatting | bytes 3145728 | tf_op args[8]
  14.8 2.6 %copy.32.weight_ref = bf16[1024,768]{1,0:T(8,128)(2,1)} copy(bf16[1024,768]{0,1:T(8,128)(2,1)} %bitcast.22) | data formatting | bytes 3145728 | tf_op jit(solution)/shard_map/reshape | solution.py:454
  17.4 0.1 broadcast_add_fusion
  17.5 0.1 add.97
  17.6 0.1 tile.21
  17.7 0.0 copy-done.7
  17.7 0.5 convert_reduce_fusion
  18.2 0.1 copy.33.ends_ref
  18.3 0.0 copy-start.1
  18.4 1.1 fusion.7
  19.5 0.3 copy-done.1
  19.8 1.6 copy-done.3
  21.4 1.0 copy-done.4
  22.4 0.8 copy-done.5
  23.2 74.6 %project.1 = (f32[256,1024]{1,0:T(8,128)S(1)}, bf16[8,4,128,256]{3,2,1,0:T(8,128)(2,1)S(1)}, bf16[8,2,64,256]{3,2,1,0:T(8,128)(2,1)S(1)}) custom-call(bf16[256,896]{1,0:T(8,128)(2,1)S(1)} %copy-done.4, bf16[896,1024]{1,0:T(8,128)(2,1)S(1)} %copy-done.3, bf16[256,128]{1,0:T(8,128)(2,1)S(1)} %pad.8.mixed_ref, bf16[128,1024]{1,0:T(8,128)(2,1)S(1)} %pad.9.lift_ref, ...), custom_call_target="tpu_custom_call" | custom-call | tf_op jit(solution)/shard_map/project/pallas_call | solution.py:423
  97.8 0.2 select_reduce_fusion
  98.0 70.7 %attend.1 = bf16[16,64,256]{2,1,0:T(8,128)(2,1)S(1)} custom-call(s32[16]{0:T(128)S(1)} %get-tuple-element.12.natural_ref, s32[16]{0:T(128)S(1)} %get-tuple-element.11.place_ref, s32[16]{0:T(128)S(1)} %multiply_add_fusion.first_ref, s32[128,1]{1,0:T(8,128)S(1)} %copy.33.ends_ref, bf16[16,64,256]{2,1,0:T(8,128)(2,1)S(1)} %bitcast.21, ...), custom_call_target="tpu_custom_call" | custom-call | tf_op jit(solution)/shard_map/attend/pallas_call | solution.py:474
  168.7 0.8 copy-done.2
  169.5 21.8 %give_back.1 = bf16[16,64,256]{2,1,0:T(8,128)(2,1)} custom-call(bf16[8,2,64,256]{3,2,1,0:T(8,128)(2,1)} %bitcast.20), custom_call_target="tpu_custom_call" | custom-call | tf_op jit(solution)/shard_map/give_back/pallas_call | solution.py:502
  191.3 0.0 all-gather.2.cloned.1.call-done
  191.3 0.0 copy-start.6
  191.3 2.6 %fusion.6 = (f32[256]{0:T(256)S(1)}, f32[256,1024]{1,0:T(8,128)S(1)}) fusion(f32[256,1024]{1,0:T(8,128)S(1)} %get-tuple-element.8, bf16[1024,256]{1,0:T(8,128)(2,1)} %bitcast.23, bf16[1024,1024]{1,0:T(8,128)(2,1)} %all-gather.2.cloned.1.call-done), kind=kOutput, calls=%fused_computation.32 | convolution fusion | flops 537394944 | bytes 4719616 | tf_op jit(solution)/shard_map/dot_general | solution.py:512
  193.9 0.3 multiply_reduce_fusion
  194.2 1.0 fusion
  (21 shorter events, 0.2 us)
Async XLA Ops:
  6.5 11.8 %copy-start = (f32[256,2048]{1,0:T(8,128)S(1)}, f32[256,2048]{1,0:T(8,128)}, u32[]{:S(2)}) copy-start(f32[256,2048]{1,0:T(8,128)} %param.20) | copy-start | bytes 6291460
  6.5 184.7 %all-gather.2.cloned.1.call-start = ((), (), s32[]{:S(2)}) async-start(), calls=%async_computation | async-start | bytes 2621440 | tf_op jit(solution)/shard_map/all_gather | solution.py:417
  14.8 2.9 %copy-start.7 = (s32[8192]{0:T(1024)S(1)}, s32[8192]{0:T(1024)}, u32[]{:S(2)}) copy-start(s32[8192]{0:T(1024)} %param.24) | copy-start | bytes 98308
  18.3 1.5 copy-start.1
  19.8 1.6 copy-start.3
  21.4 1.0 copy-start.4
  22.4 0.8 copy-start.5
  23.2 74.6 %copy-start.8 = (s32[16]{0:T(128)S(1)}, s32[16]{0:T(128)}, u32[]{:S(2)}) copy-start(s32[16]{0:T(128)} %param.25) | copy-start | bytes 196
  168.7 0.8 copy-start.2
  191.3 2.9 %copy-start.6 = (bf16[1024,80]{0,1:T(8,128)(2,1)S(1)}, bf16[1024,80]{0,1:T(8,128)(2,1)}, u32[]{:S(2)}) copy-start(bf16[1024,80]{0,1:T(8,128)(2,1)} %param.23) | copy-start | bytes 491524
Sparse Core Ops, SparseCore 0:
  8.9 76.1 all-gather.1

commit v2 on v1

--- a/solution.py
+++ b/solution.py
@@ -60,8 +60,7 @@
     me = lax.axis_index("seq")
     tp = lax.axis_index("tp")
     tokens = cond_buf.shape[1]
-    frames = mixed_ref.shape[0]
-    cols = heads * dim
+    frames = mixed_ref.shape[1]
 
     barrier = pltpu.get_barrier_semaphore()
     for d in range(1, tp_n):
@@ -117,6 +116,7 @@
     spread = jnp.where((frame_at >= first) & (frame_at < first + upsample), 1.0, 0.0).astype(
         jnp.bfloat16
     )
+    phase = jnp.concatenate([phase_ref[...]] * (8 // upsample), axis=0)
     q_factor = math.log2(math.e) / math.sqrt(dim)
 
     def kv_copy(chunk, d):
@@ -162,11 +162,14 @@
             mix_copy(step).wait_recv()
             cond_copy(step).wait_recv()
 
-        state = jnp.dot(mix_buf[step], lift_ref[...], preferred_element_type=jnp.float32)
+        state = lax.dot_general(
+            mix_buf[step],
+            lift_ref[...],
+            (((0,), (0,)), ((), ())),
+            preferred_element_type=jnp.float32,
+        )
         state = state + jnp.dot(spread, cond_buf[step], preferred_element_type=jnp.float32)
-        state = (
-            state.reshape(frames // 8, 8, state.shape[1]) + phase_ref[...][None]
-        ).reshape(state.shape)
+        state = (state.reshape(frames // 8, 8, state.shape[1]) + phase[None]).reshape(state.shape)
 
         @pl.when(step == 0)
         def _():
@@ -176,7 +179,7 @@
         for kind in range(3):
             made = jnp.dot(
                 normed,
-                weight_ref[:, kind * cols : (kind + 1) * cols],
+                weight_ref[kind],
                 preferred_element_type=jnp.float32,
             ).T
             if kind == 0:
@@ -223,6 +226,8 @@
     out_ref,
     key_buf,
     value_buf,
+    even_buf,
+    odd_buf,
 ):
     seq_n, tp_n, dim, block_len = dims
     frames = q_ref.shape[-1]
@@ -247,51 +252,88 @@
     ends = ends_ref[...]
     stop = jnp.min(jnp.where(ends > at, ends, 1 << 30), axis=0, keepdims=True)
 
-    def visit(carry, stored, count, limit):
+    def score(stored, count):
+        keys = key_buf[pl.ds(pl.multiple_of(stored * block_len, block_len), count), :]
+        return jnp.dot(keys, queries, preferred_element_type=jnp.float32)
+
+    def absorb(carry, *parts):
         highest, total = carry
-        keys = key_buf[pl.ds(pl.multiple_of(stored * block_len, block_len), count), :]
-        scores = jnp.dot(keys, queries, preferred_element_type=jnp.float32)
-        if limit is not None:
-            row = lax.broadcasted_iota(jnp.int32, (count, frames), 0)
-            scores = jnp.where(row < limit, scores, masked_score)
-        above = jnp.maximum(highest, jnp.max(scores, axis=0, keepdims=True))
-        expo = jnp.exp2(scores - above).astype(jnp.bfloat16)
+        above = highest
+        for scores, _ in parts:
+            above = jnp.maximum(above, jnp.max(scores, axis=0, keepdims=True))
         total = total * jnp.exp2(highest - above)
-        for c in range(pl.cdiv(count, frames)):
-            size = min(frames, count - c * frames)
-            total = total + jnp.dot(
-                value_buf[stored * per_block + c, :, :size],
-                expo[c * frames : c * frames + size],
-                preferred_element_type=jnp.float32,
-            )
+        for scores, stored in parts:
+            count = scores.shape[0]
+            expo = jnp.exp2((scores - above)).astype(jnp.bfloat16)
+            for c in range(pl.cdiv(count, frames)):
+                size = min(frames, count - c * frames)
+                total = total + jnp.dot(
+                    value_buf[stored * per_block + c, :, :size],
+                    expo[c * frames : c * frames + size],
+                    preferred_element_type=jnp.float32,
+                )
         return above, total
+
+    def masked(scores, limit):
+        row = lax.broadcasted_iota(jnp.int32, scores.shape, 0)
+        return jnp.where(row < limit, scores, masked_score)
 
     carry = (
         jnp.full((1, frames), masked_score, jnp.float32),
         jnp.zeros((value_rows, frames), jnp.float32),
     )
-    carry = visit(carry, place_ref[natural], block_len, stop - base)
-    beyond = jnp.minimum(natural + 1, block_count - 1)
-    carry = visit(
-        carry,
-        place_ref[beyond],
-        128,
-        jnp.where(natural + 1 < block_count, stop - base - block_len, 0),
+    here = place_ref[natural]
+    beyond = place_ref[jnp.minimum(natural + 1, block_count - 1)]
+    over = jnp.where(natural + 1 < block_count, stop - base - block_len, 0)
+    here_scores = score(here, block_len)
+    beyond_scores = score(beyond, 128)
+    even_buf[...] = score(place_ref[0], block_len)
+    carry = absorb(
+        carry, (masked(here_scores, stop - base), here), (masked(beyond_scores, over), beyond)
     )
 
     def pair(i, carry):
-        carry = visit(carry, place_ref[2 * i], block_len, None)
-        return visit(carry, place_ref[2 * i + 1], block_len, None)
+        odd_buf[...] = score(place_ref[2 * i + 1], block_len)
+        carry = absorb(carry, (even_buf[...], place_ref[2 * i]))
+        even_buf[...] = score(place_ref[2 * i + 2], block_len)
+        return absorb(carry, (odd_buf[...], place_ref[2 * i + 1]))
 
     carry = lax.fori_loop(0, natural // 2, pair, carry)
+    last = natural - lax.rem(natural, 2)
     carry = lax.fori_loop(
-        2 * (natural // 2),
-        natural,
-        lambda j, carry: visit(carry, place_ref[j], block_len, None),
-        carry,
+        last, natural, lambda j, carry: absorb(carry, (even_buf[...], place_ref[j])), carry
     )
     total = carry[1]
     out_ref[0] = (total[:dim] / total[dim : dim + 1]).astype(jnp.bfloat16)
+
+
+def attend_call(dims, natural, place, first, ends, queries, keys_values):
+    block_len = dims[3]
+    tiles, dim, frames = queries.shape
+    chunks = keys_values.shape[0]
+    scores = pltpu.VMEM((block_len, frames), jnp.float32)
+    return pl.pallas_call(
+        functools.partial(attend_kernel, dims),
+        out_shape=jax.ShapeDtypeStruct((tiles, dim, frames), jnp.bfloat16),
+        grid_spec=pltpu.PrefetchScalarGridSpec(
+            num_scalar_prefetch=3,
+            grid=(tiles,),
+            in_specs=[
+                pl.BlockSpec(memory_space=pltpu.VMEM),
+                pl.BlockSpec((1, dim, frames), lambda i, *_: (i, 0, 0)),
+                pl.BlockSpec(memory_space=pltpu.VMEM),
+            ],
+            out_specs=pl.BlockSpec((1, dim, frames), lambda i, *_: (i, 0, 0)),
+            scratch_shapes=[
+                pltpu.VMEM((chunks * frames, dim), jnp.bfloat16),
+                pltpu.VMEM((chunks, dim + 16, frames), jnp.bfloat16),
+                scores,
+                scores,
+            ],
+        ),
+        compiler_params=pltpu.CompilerParams(vmem_limit_bytes=40 << 20),
+        name="attend",
+    )(natural, place, first, ends, queries, keys_values)
 
 
 def return_kernel(dims, att_ref, out_ref, send_sem, recv_sem):
@@ -407,14 +449,9 @@
     me = lax.axis_index("seq")
 
     moment = timestep[0]
-    mixed = ((1.0 - moment) * noise + moment * target_spectrum).astype(jnp.bfloat16)
-    padding = -bins % 128
-    mixed = jnp.pad(mixed, ((0, 0), (0, padding)))
-    lift = jnp.pad(frame_lift, ((0, padding), (0, 0)))
+    mixed = ((1.0 - moment) * noise.T + moment * target_spectrum.T).astype(jnp.bfloat16)
     modulation = time_modulation(timestep, time_weight)
     mod = jnp.stack([modulation[:width], 1.0 + modulation[width:]])
-    phase = jnp.tile(phase_offsets, (8 // upsample, 1))
-    mixing = lax.all_gather(head_mixing, "tp", axis=0, tiled=True)
 
     vmem = pl.BlockSpec(memory_space=pltpu.VMEM)
     hbm = pl.BlockSpec(memory_space=pl.ANY)
@@ -433,7 +470,7 @@
             pltpu.VMEM((tp_n, tokens, width), bf16),
             pltpu.VMEM((tp_n, tokens, width), bf16),
             pltpu.VMEM((tp_n, tokens, width), bf16),
-            pltpu.VMEM((tp_n, frame_count, bins + padding), bf16),
+            pltpu.VMEM((tp_n, bins, frame_count), bf16),
             pltpu.VMEM((tp_n, heads, 2 * dim, frame_count), bf16),
             pltpu.VMEM((tp_n, heads, dim, frame_count), bf16),
         ]
@@ -448,11 +485,14 @@
         semantic_states,
         token_projection,
         mixed,
-        lift,
-        phase,
+        frame_lift,
+        phase_offsets,
         mod,
-        attention_weight.reshape(width, 3 * cols),
-    )
+        attention_weight.transpose(1, 0, 2),
+    )
+
+    head_mixing, q_all = lax.optimization_barrier((head_mixing, q_all))
+    mixing = lax.all_gather(head_mixing, "tp", axis=0, tiled=True)
 
     group_ids = jnp.arange(frames_total // 64, dtype=jnp.int32)
     ends = jnp.sum((group_index[None, :] <= group_ids[:, None]).astype(jnp.int32), axis=1)[:, None]
@@ -471,26 +511,8 @@
     first = natural * block_len + jnp.tile(owner * frame_count % block_len, seq_n)
 
     tiles = seq_n * per
-    attended = pl.pallas_call(
-        functools.partial(attend_kernel, (seq_n, tp_n, dim, block_len)),
-        out_shape=jax.ShapeDtypeStruct((tiles, dim, frame_count), bf16),
-        grid_spec=pltpu.PrefetchScalarGridSpec(
-            num_scalar_prefetch=3,
-            grid=(tiles,),
-            in_specs=[
-                vmem,
-                pl.BlockSpec((1, dim, frame_count), lambda i, *_: (i, 0, 0)),
-                vmem,
-            ],
-            out_specs=pl.BlockSpec((1, dim, frame_count), lambda i, *_: (i, 0, 0)),
-            scratch_shapes=[
-                pltpu.VMEM((frames_total, dim), bf16),
-                pltpu.VMEM((seq_n * tp_n, dim + 16, frame_count), bf16),
-            ],
-        ),
-        compiler_params=pltpu.CompilerParams(vmem_limit_bytes=40 << 20),
-        name="attend",
-    )(
+    attended = attend_call(
+        (seq_n, tp_n, dim, block_len),
         natural,
         place,
         first,

time: 203 us -> 146 us (0.72)
  Pallas kernels: 167 us -> 115 us
  local copies, waits for them, and re-layouts: 14.2 us -> 10.4 us
    pallas_call x1, Pallas kernels: 70.7 us -> 44.8 us  [attend_call(): pl.pallas_call(functools.partial(attend_kernel, dims), out_shape=jax.Shap...]
    pallas_call x1, Pallas kernels: 74.6 us -> 50.5 us  [body(): pl.pallas_call(functools.partial(project_kernel, (seq_n, tp_n, heads, ran...]
    reshape x1 -> x0, local copies, waits for them, and re-layouts: 2.59 us -> none  [body(): attention_weight.reshape(width, 3 * cols)]
    unnamed x21 -> x32, local copies, waits for them, and re-layouts: 9.04 us -> 10.2 us
  transfers between devices with their start and end apart: 1 -> 1, of which waited for: 0 -> 0; matrix products, arithmetic and copies ran while one was open for 6% -> 1% of each run, Pallas kernels for 83% -> 44%
where the time goes in v2:
time: 146 us
  Pallas kernels  115 us (79%)
  between operations  14.4 us (10%)
  local copies, waits for them, and re-layouts  10.4 us (7%)
  matrix products  4.71 us (3%)
    pallas_call x1, Pallas kernels, body(): pl.pallas_call(functools.partial(project_kernel, (seq_n, tp_n, heads, ran...  50.5 us
    pallas_call x1, Pallas kernels, attend_call(): pl.pallas_call(functools.partial(attend_kernel, dims), out_shape=jax.Shap...  44.8 us
    pallas_call x1, Pallas kernels, body(): pl.pallas_call(functools.partial(return_kernel, (seq_n, tp_n, heads, rank...  19.7 us
    unnamed x32, local copies, waits for them, and re-layouts  10.2 us
  transfers between devices with their start and end apart: 1, of which 0 were waited for; matrix products, arithmetic and copies ran while one was open for 1% of the time, Pallas kernels for 44%

profile of v2, /device:TPU:0, one launch (start us, length us, event | category | flops | bytes accessed | tf_op | source)
XLA Modules:
  0.0 145.8 jit_solution(17198937216114782827)
XLA Ops:
  6.5 0.0 copy-start
  6.5 0.0 all-gather.2.cloned.1.call-start
  7.5 0.7 copy-done
  8.1 1.1 fusion.8
  9.3 0.0 copy-done.13
  9.3 0.0 copy-done.12
  9.3 0.0 copy-done.9
  9.3 0.0 copy-done.10
  9.3 0.0 copy-start.4
  9.3 1.5 %copy-done.4 = bf16[896,1024]{1,0:T(8,128)(2,1)S(1)} copy-done((bf16[896,1024]{1,0:T(8,128)(2,1)S(1)}, bf16[896,1024]{1,0:T(8,128)(2,1)}, u32[]{:S(2)}) %copy-start.4) | copy-done | bytes 1835032
  10.8 1.4 copy-done.5
  12.2 1.0 copy-done.8
  13.3 50.5 %project.1 = (f32[256,1024]{1,0:T(8,128)S(1)}, bf16[8,4,128,256]{3,2,1,0:T(8,128)(2,1)S(1)}, bf16[8,2,64,256]{3,2,1,0:T(8,128)(2,1)S(1)}) custom-call(bf16[256,896]{1,0:T(8,128)(2,1)S(1)} %copy-done.8, bf16[896,1024]{1,0:T(8,128)(2,1)S(1)} %copy-done.4, bf16[80,256]{1,0:T(8,128)(2,1)S(1)} %fusion.3.mixed_ref, bf16[80,1024]{1,0:T(8,128)(2,1)S(1)} %copy-done.9, ...), custom_call_target="tpu_custom_call" | custom-call | tf_op jit(solution)/shard_map/project/pallas_call | solution.py:460
  63.8 1.3 copy-done.1
  65.1 0.8 copy-done.6
  65.9 0.0 all-gather.2.cloned.1.call-update
  66.0 0.1 tile.10
  66.1 0.1 broadcast_add_fusion
  66.1 0.1 add.94
  66.2 0.5 convert_reduce_fusion
  66.7 0.1 copy.16.ends_ref
  66.8 0.2 select_reduce_fusion
  67.0 1.6 %copy-done.2 = bf16[8,4,128,256]{3,2,1,0:T(8,128)(2,1)S(1)} copy-done((bf16[8,4,128,256]{3,2,1,0:T(8,128)(2,1)S(1)}, bf16[8,4,128,256]{3,2,1,0:T(8,128)(2,1)}, u32[]{:S(2)}) %copy-start.2) | copy-done | bytes 2097176
  68.6 1.0 copy-done.7
  69.7 44.8 %attend.1 = bf16[16,64,256]{2,1,0:T(8,128)(2,1)S(1)} custom-call(s32[16]{0:T(128)S(1)} %get-tuple-element.16.natural_ref, s32[16]{0:T(128)S(1)} %get-tuple-element.15.place_ref, s32[16]{0:T(128)S(1)} %multiply_add_fusion.first_ref, s32[128,1]{1,0:T(8,128)S(1)} %copy.16.ends_ref, bf16[16,64,256]{2,1,0:T(8,128)(2,1)S(1)} %bitcast.24, ...), custom_call_target="tpu_custom_call" | custom-call | tf_op jit(solution)/shard_map/attend/pallas_call | solution.py:315
  114.5 0.8 copy-done.3
  115.3 19.7 %give_back.1 = bf16[16,64,256]{2,1,0:T(8,128)(2,1)} custom-call(bf16[8,2,64,256]{3,2,1,0:T(8,128)(2,1)} %bitcast.22), custom_call_target="tpu_custom_call" | custom-call | tf_op jit(solution)/shard_map/give_back/pallas_call | solution.py:524
  135.0 0.0 all-gather.2.cloned.1.call-done
  135.1 0.0 copy-start.11
  135.1 2.6 %fusion.7 = (f32[256]{0:T(256)S(1)}, f32[256,1024]{1,0:T(8,128)S(1)}) fusion(f32[256,1024]{1,0:T(8,128)S(1)} %get-tuple-element.10, bf16[1024,256]{1,0:T(8,128)(2,1)} %bitcast.25, bf16[1024,1024]{1,0:T(8,128)(2,1)} %all-gather.2.cloned.1.call-done), kind=kOutput, calls=%fused_computation.33 | convolution fusion | flops 537394944 | bytes 4719616 | tf_op jit(solution)/shard_map/dot_general | solution.py:534
  137.7 0.3 multiply_reduce_fusion
  138.0 1.0 fusion
  (27 shorter events, 0.2 us)
Async XLA Ops:
  6.5 1.6 %copy-start = (f32[256,2048]{1,0:T(8,128)S(1)}, f32[256,2048]{1,0:T(8,128)}, u32[]{:S(2)}) copy-start(f32[256,2048]{1,0:T(8,128)} %param.20) | copy-start | bytes 6291460
  6.5 2.7 %copy-start.13 = (f32[256,80]{0,1:T(8,128)S(1)}, f32[256,80]{0,1:T(8,128)}, u32[]{:S(2)}) copy-start(f32[256,80]{0,1:T(8,128)} %param.17) | copy-start | bytes 245764
  6.5 2.7 %copy-start.12 = (f32[256,80]{0,1:T(8,128)S(1)}, f32[256,80]{0,1:T(8,128)}, u32[]{:S(2)}) copy-start(f32[256,80]{0,1:T(8,128)} %param.16) | copy-start | bytes 245764
  6.5 2.8 %copy-start.9 = (bf16[80,1024]{1,0:T(8,128)(2,1)S(1)}, bf16[80,1024]{1,0:T(8,128)(2,1)}, u32[]{:S(2)}) copy-start(bf16[80,1024]{1,0:T(8,128)(2,1)} %lift_ref.1) | copy-start | bytes 491524
  6.5 2.8 %copy-start.10 = (f32[4,1024]{1,0:T(4,128)S(1)}, f32[4,1024]{1,0:T(4,128)}, u32[]{:S(2)}) copy-start(f32[4,1024]{1,0:T(4,128)} %phase_ref.1) | copy-start | bytes 49156
  6.5 128.5 %all-gather.2.cloned.1.call-start = ((), (), s32[]{:S(2)}) async-start(), calls=%async_computation | async-start | bytes 2621440 | tf_op jit(solution)/shard_map/all_gather | solution.py:495
  9.3 1.5 %copy-start.4 = (bf16[896,1024]{1,0:T(8,128)(2,1)S(1)}, bf16[896,1024]{1,0:T(8,128)(2,1)}, u32[]{:S(2)}) copy-start(bf16[896,1024]{1,0:T(8,128)(2,1)} %proj_ref.1) | copy-start | bytes 5505028
  10.8 1.4 copy-start.5
  12.2 1.0 copy-start.8
  13.3 53.0 %copy-start.14 = (s32[8192]{0:T(1024)S(1)}, s32[8192]{0:T(1024)}, u32[]{:S(2)}) copy-start(s32[8192]{0:T(1024)} %param.24) | copy-start | bytes 98308
  13.3 53.6 %copy-start.15 = (s32[16]{0:T(128)S(1)}, s32[16]{0:T(128)}, u32[]{:S(2)}) copy-start(s32[16]{0:T(128)} %param.25) | copy-start | bytes 196
  63.8 1.3 copy-start.1
  65.1 0.8 copy-start.6
  67.0 1.6 %copy-start.2 = (bf16[8,4,128,256]{3,2,1,0:T(8,128)(2,1)S(1)}, bf16[8,4,128,256]{3,2,1,0:T(8,128)(2,1)}, u32[]{:S(2)}) copy-start(bf16[8,4,128,256]{3,2,1,0:T(8,128)(2,1)} %copy-done.1) | copy-start | bytes 6291460
  68.6 1.0 copy-start.7
  114.5 0.8 copy-start.3
  135.1 2.9 %copy-start.11 = (bf16[1024,80]{0,1:T(8,128)(2,1)S(1)}, bf16[1024,80]{0,1:T(8,128)(2,1)}, u32[]{:S(2)}) copy-start(bf16[1024,80]{0,1:T(8,128)(2,1)} %param.23) | copy-start | bytes 491524
Sparse Core Ops, SparseCore 0:
  66.1 49.7 all-gather.1

commit v3 on v2

--- a/solution.py
+++ b/solution.py
@@ -53,6 +53,8 @@
     mix_recv,
     kv_send,
     kv_recv,
+    share_send,
+    share_recv,
     q_send,
     q_recv,
 ):
@@ -119,14 +121,28 @@
     phase = jnp.concatenate([phase_ref[...]] * (8 // upsample), axis=0)
     q_factor = math.log2(math.e) / math.sqrt(dim)
 
+    head = me // ranks
+    rank = lax.rem(me, ranks)
+
     def kv_copy(chunk, d):
-        dest = lax.rem(me + d, seq_n)
+        goal = lax.rem(head + d, heads)
         return pltpu.make_async_remote_copy(
-            src_ref=kv_buf.at[chunk, dest // ranks],
+            src_ref=kv_buf.at[chunk, goal],
             dst_ref=kv_all.at[me, chunk],
             send_sem=kv_send.at[d, chunk],
             recv_sem=kv_recv.at[d, chunk],
-            device_id=(dest, tp),
+            device_id=(goal * ranks + rank, tp),
+            device_id_type=MESH,
+        )
+
+    def share_copy(chunk, d, j):
+        source = lax.rem(head - d + heads, heads) * ranks + rank
+        return pltpu.make_async_remote_copy(
+            src_ref=kv_all.at[source, chunk] if d else kv_buf.at[chunk, head],
+            dst_ref=kv_all.at[source, chunk],
+            send_sem=share_send.at[d * ranks + j, chunk],
+            recv_sem=share_recv.at[d * ranks + j, chunk],
+            device_id=(head * ranks + lax.rem(rank + j, ranks), tp),
             device_id_type=MESH,
         )
 
@@ -188,8 +204,11 @@
                 kv_buf[chunk, :, (kind - 1) * dim : kind * dim, :] = made.astype(
                     jnp.bfloat16
                 ).reshape(heads, dim, frames)
+        for d in range(1, heads):
+            kv_copy(chunk, d).start()
+        for j in range(1, ranks):
+            share_copy(chunk, 0, j).start()
         for d in range(1, seq_n):
-            kv_copy(chunk, d).start()
 
             @pl.when(lax.rem(chunk, ranks) == lax.rem(lax.rem(me + d, seq_n), ranks))
             def _():
@@ -200,6 +219,13 @@
         @pl.when(lax.rem(chunk, ranks) == lax.rem(me, ranks))
         def _():
             own_q(chunk).start()
+
+    for step in range(tp_n):
+        chunk = lax.rem(tp - step + tp_n, tp_n)
+        for d in range(1, heads):
+            kv_copy(chunk, d).wait_recv()
+            for j in range(1, ranks):
+                share_copy(chunk, d, j).start()
 
     for d in range(1, tp_n):
         mix_copy(d).wait_send()
@@ -207,8 +233,11 @@
         cond_copy(d).wait_send()
     for chunk in range(tp_n):
         own_kv(chunk).wait()
-        for d in range(1, seq_n):
-            kv_copy(chunk, d).wait()
+        for d in range(1, heads):
+            kv_copy(chunk, d).wait_send()
+        for d in range(heads):
+            for j in range(1, ranks):
+                share_copy(chunk, d, j).wait()
     for k in range(tp_n // ranks):
         own_q(k * ranks).wait()
         for d in range(1, seq_n):
@@ -475,7 +504,8 @@
             pltpu.VMEM((tp_n, heads, dim, frame_count), bf16),
         ]
         + [dma((tp_n,))] * 6
-        + [dma((seq_n, tp_n))] * 2
+        + [dma((heads, tp_n))] * 2
+        + [dma((heads * ranks, tp_n))] * 2
         + [dma((seq_n, per))] * 2,
         compiler_params=pltpu.CompilerParams(
             collective_id=0, has_side_effects=True, vmem_limit_bytes=40 << 20
@@ -491,7 +521,7 @@
         attention_weight.transpose(1, 0, 2),
     )
 
-    head_mixing, q_all = lax.optimization_barrier((head_mixing, q_all))
+    head_mixing, start_state = lax.optimization_barrier((head_mixing, start_state))
     mixing = lax.all_gather(head_mixing, "tp", axis=0, tiled=True)
 
     group_ids = jnp.arange(frames_total // 64, dtype=jnp.int32)

time: 146 us -> 139 us (0.952)
  Pallas kernels: 115 us -> 108 us
    pallas_call x1, Pallas kernels: 50.5 us -> 43.1 us  [body(): pl.pallas_call(functools.partial(project_kernel, (seq_n, tp_n, heads, ran...]
  transfers between devices with their start and end apart: 1 -> 1, of which waited for: 0 -> 0; matrix products, arithmetic and copies ran while one was open for 1% -> 1% of each run, Pallas kernels for 44% -> 47%
where the time goes in v3:
time: 139 us
  Pallas kernels  108 us (78%)
  between operations  14.4 us (10%)
  local copies, waits for them, and re-layouts  10.4 us (7%)
  matrix products  4.71 us (3%)
    pallas_call x1, Pallas kernels, attend_call(): pl.pallas_call(functools.partial(attend_kernel, dims), out_shape=jax.Shap...  44.8 us
    pallas_call x1, Pallas kernels, body(): pl.pallas_call(functools.partial(project_kernel, (seq_n, tp_n, heads, ran...  43.1 us
    pallas_call x1, Pallas kernels, body(): pl.pallas_call(functools.partial(return_kernel, (seq_n, tp_n, heads, rank...  20.5 us
    unnamed x32, local copies, waits for them, and re-layouts  10.2 us
  transfers between devices with their start and end apart: 1, of which 0 were waited for; matrix products, arithmetic and copies ran while one was open for 1% of the time, Pallas kernels for 47%

profile of v3, /device:TPU:0, one launch (start us, length us, event | category | flops | bytes accessed | tf_op | source)
XLA Modules:
  0.0 139.1 jit_solution(1543745309942782339)
XLA Ops:
  6.5 0.0 copy-start
  6.5 0.0 all-gather.2.cloned.1.call-start
  7.5 0.7 copy-done
  8.1 1.1 fusion.8
  9.3 0.0 copy-done.13
  9.3 0.0 copy-done.12
  9.3 0.0 copy-done.9
  9.3 0.0 copy-start.4
  9.3 1.5 %copy-done.4 = bf16[896,1024]{1,0:T(8,128)(2,1)S(1)} copy-done((bf16[896,1024]{1,0:T(8,128)(2,1)S(1)}, bf16[896,1024]{1,0:T(8,128)(2,1)}, u32[]{:S(2)}) %copy-start.4) | copy-done | bytes 1835032
  10.8 1.4 %copy-done.5 = bf16[1024,3,256]{2,0,1:T(8,128)(2,1)S(1)} copy-done((bf16[1024,3,256]{2,0,1:T(8,128)(2,1)S(1)}, bf16[1024,3,256]{2,0,1:T(8,128)(2,1)}, u32[]{:S(2)}) %copy-start.5) | copy-done | bytes 1572888
  12.2 1.0 copy-done.8
  13.3 43.1 %project.1 = (f32[256,1024]{1,0:T(8,128)S(1)}, bf16[8,4,128,256]{3,2,1,0:T(8,128)(2,1)S(1)}, bf16[8,2,64,256]{3,2,1,0:T(8,128)(2,1)S(1)}) custom-call(bf16[256,896]{1,0:T(8,128)(2,1)S(1)} %copy-done.8, bf16[896,1024]{1,0:T(8,128)(2,1)S(1)} %copy-done.4, bf16[80,256]{1,0:T(8,128)(2,1)S(1)} %fusion.3.mixed_ref, bf16[80,1024]{1,0:T(8,128)(2,1)S(1)} %copy-done.9, ...), custom_call_target="tpu_custom_call" | custom-call | tf_op jit(solution)/shard_map/project/pallas_call | solution.py:489
  56.3 1.3 copy-done.1
  57.7 0.8 copy-done.6
  58.5 0.0 all-gather.2.cloned.1.call-update
  58.5 0.1 tile.10
  58.6 0.1 broadcast_add_fusion
  58.7 0.1 add.94
  58.8 0.5 convert_reduce_fusion
  59.3 0.1 copy.16.ends_ref
  59.4 0.2 select_reduce_fusion
  59.6 1.6 %copy-done.2 = bf16[8,4,128,256]{3,2,1,0:T(8,128)(2,1)S(1)} copy-done((bf16[8,4,128,256]{3,2,1,0:T(8,128)(2,1)S(1)}, bf16[8,4,128,256]{3,2,1,0:T(8,128)(2,1)}, u32[]{:S(2)}) %copy-start.2) | copy-done | bytes 2097176
  61.2 1.0 copy-done.7
  62.2 44.8 %attend.1 = bf16[16,64,256]{2,1,0:T(8,128)(2,1)S(1)} custom-call(s32[16]{0:T(128)S(1)} %get-tuple-element.16.natural_ref, s32[16]{0:T(128)S(1)} %get-tuple-element.15.place_ref, s32[16]{0:T(128)S(1)} %multiply_add_fusion.first_ref, s32[128,1]{1,0:T(8,128)S(1)} %copy.16.ends_ref, bf16[16,64,256]{2,1,0:T(8,128)(2,1)S(1)} %bitcast.24, ...), custom_call_target="tpu_custom_call" | custom-call | tf_op jit(solution)/shard_map/attend/pallas_call | solution.py:344
  107.0 0.8 copy-done.3
  107.8 20.5 %give_back.1 = bf16[16,64,256]{2,1,0:T(8,128)(2,1)} custom-call(bf16[8,2,64,256]{3,2,1,0:T(8,128)(2,1)} %bitcast.22), custom_call_target="tpu_custom_call" | custom-call | tf_op jit(solution)/shard_map/give_back/pallas_call | solution.py:554
  128.3 0.0 all-gather.2.cloned.1.call-done
  128.3 0.0 copy-start.11
  128.3 2.6 %fusion.7 = (f32[256]{0:T(256)S(1)}, f32[256,1024]{1,0:T(8,128)S(1)}) fusion(f32[256,1024]{1,0:T(8,128)S(1)} %get-tuple-element.11, bf16[1024,256]{1,0:T(8,128)(2,1)} %bitcast.25, bf16[1024,1024]{1,0:T(8,128)(2,1)} %all-gather.2.cloned.1.call-done), kind=kOutput, calls=%fused_computation.33 | convolution fusion | flops 537394944 | bytes 4719616 | tf_op jit(solution)/shard_map/dot_general | solution.py:564
  131.0 0.3 multiply_reduce_fusion
  131.2 0.0 copy-done.11
  131.2 1.0 fusion
  (27 shorter events, 0.2 us)
Async XLA Ops:
  6.5 1.6 %copy-start = (f32[256,2048]{1,0:T(8,128)S(1)}, f32[256,2048]{1,0:T(8,128)}, u32[]{:S(2)}) copy-start(f32[256,2048]{1,0:T(8,128)} %param.20) | copy-start | bytes 6291460
  6.5 2.7 %copy-start.13 = (f32[256,80]{0,1:T(8,128)S(1)}, f32[256,80]{0,1:T(8,128)}, u32[]{:S(2)}) copy-start(f32[256,80]{0,1:T(8,128)} %param.17) | copy-start | bytes 245764
  6.5 2.7 %copy-start.12 = (f32[256,80]{0,1:T(8,128)S(1)}, f32[256,80]{0,1:T(8,128)}, u32[]{:S(2)}) copy-start(f32[256,80]{0,1:T(8,128)} %param.16) | copy-start | bytes 245764
  6.5 2.8 %copy-start.9 = (bf16[80,1024]{1,0:T(8,128)(2,1)S(1)}, bf16[80,1024]{1,0:T(8,128)(2,1)}, u32[]{:S(2)}) copy-start(bf16[80,1024]{1,0:T(8,128)(2,1)} %lift_ref.1) | copy-start | bytes 491524
  6.5 2.8 %copy-start.10 = (f32[4,1024]{1,0:T(4,128)S(1)}, f32[4,1024]{1,0:T(4,128)}, u32[]{:S(2)}) copy-start(f32[4,1024]{1,0:T(4,128)} %phase_ref.1) | copy-start | bytes 49156
  6.5 121.8 %all-gather.2.cloned.1.call-start = ((), (), s32[]{:S(2)}) async-start(), calls=%async_computation | async-start | bytes 2621440 | tf_op jit(solution)/shard_map/all_gather | solution.py:525
  9.3 1.5 %copy-start.4 = (bf16[896,1024]{1,0:T(8,128)(2,1)S(1)}, bf16[896,1024]{1,0:T(8,128)(2,1)}, u32[]{:S(2)}) copy-start(bf16[896,1024]{1,0:T(8,128)(2,1)} %proj_ref.1) | copy-start | bytes 5505028
  10.8 1.4 %copy-start.5 = (bf16[1024,3,256]{2,0,1:T(8,128)(2,1)S(1)}, bf16[1024,3,256]{2,0,1:T(8,128)(2,1)}, u32[]{:S(2)}) copy-start(bf16[1024,3,256]{2,0,1:T(8,128)(2,1)} %param.21) | copy-start | bytes 4718596
  12.2 1.0 copy-start.8
  13.3 45.5 %copy-start.14 = (s32[8192]{0:T(1024)S(1)}, s32[8192]{0:T(1024)}, u32[]{:S(2)}) copy-start(s32[8192]{0:T(1024)} %param.24) | copy-start | bytes 98308
  13.3 46.1 %copy-start.15 = (s32[16]{0:T(128)S(1)}, s32[16]{0:T(128)}, u32[]{:S(2)}) copy-start(s32[16]{0:T(128)} %param.25) | copy-start | bytes 196
  56.3 1.3 copy-start.1
  57.7 0.8 copy-start.6
  59.6 1.6 %copy-start.2 = (bf16[8,4,128,256]{3,2,1,0:T(8,128)(2,1)S(1)}, bf16[8,4,128,256]{3,2,1,0:T(8,128)(2,1)}, u32[]{:S(2)}) copy-start(bf16[8,4,128,256]{3,2,1,0:T(8,128)(2,1)} %copy-done.1) | copy-start | bytes 6291460
  61.2 1.0 copy-start.7
  107.0 0.8 copy-start.3
  128.3 2.9 %copy-start.11 = (bf16[1024,80]{0,1:T(8,128)(2,1)S(1)}, bf16[1024,80]{0,1:T(8,128)(2,1)}, u32[]{:S(2)}) copy-start(bf16[1024,80]{0,1:T(8,128)(2,1)} %param.23) | copy-start | bytes 491524
Sparse Core Ops, SparseCore 0:
  58.6 49.7 all-gather.1

commit v4 on v3

--- a/solution.py
+++ b/solution.py
@@ -267,7 +267,7 @@
 
     @pl.when(tile == 0)
     def _():
-        @pl.loop(0, seq_n * tp_n)
+        @pl.loop(0, seq_n * tp_n, unroll=4)
         def _(i):
             at = pl.ds(pl.multiple_of(i * frames, frames), frames)
             key_buf[at, :] = kv_ref[i, :dim, :].astype(jnp.float32).T.astype(jnp.bfloat16)

time: 139 us -> 137 us (0.986)
  Pallas kernels: 108 us -> 106 us
    pallas_call x1, Pallas kernels: 44.8 us -> 42.7 us  [attend_call(): pl.pallas_call(functools.partial(attend_kernel, dims), out_shape=jax.Shap...]
  transfers between devices with their start and end apart: 1 -> 1, of which waited for: 0 -> 0; matrix products, arithmetic and copies ran while one was open for 1% -> 1% of each run, Pallas kernels for 47% -> 46%
where the time goes in v4:
time: 137 us
  Pallas kernels  106 us (77%)
  between operations  14.4 us (11%)
  local copies, waits for them, and re-layouts  10.4 us (8%)
  matrix products  4.72 us (3%)
    pallas_call x1, Pallas kernels, body(): pl.pallas_call(functools.partial(project_kernel, (seq_n, tp_n, heads, ran...  43.1 us
    pallas_call x1, Pallas kernels, attend_call(): pl.pallas_call(functools.partial(attend_kernel, dims), out_shape=jax.Shap...  42.7 us
    pallas_call x1, Pallas kernels, body(): pl.pallas_call(functools.partial(return_kernel, (seq_n, tp_n, heads, rank...  20.4 us
    unnamed x32, local copies, waits for them, and re-layouts  10.2 us
  transfers between devices with their start and end apart: 1, of which 0 were waited for; matrix products, arithmetic and copies ran while one was open for 1% of the time, Pallas kernels for 46%

profile of v4, /device:TPU:0, one launch (start us, length us, event | category | flops | bytes accessed | tf_op | source)
XLA Modules:
  0.0 137.0 jit_solution(381891396534863340)
XLA Ops:
  6.5 0.0 copy-start
  6.5 0.0 all-gather.2.cloned.1.call-start
  7.5 0.7 copy-done
  8.1 1.1 fusion.8
  9.3 0.0 copy-done.13
  9.3 0.0 copy-done.12
  9.3 0.0 copy-done.9
  9.3 0.0 copy-start.4
  9.3 1.5 %copy-done.4 = bf16[896,1024]{1,0:T(8,128)(2,1)S(1)} copy-done((bf16[896,1024]{1,0:T(8,128)(2,1)S(1)}, bf16[896,1024]{1,0:T(8,128)(2,1)}, u32[]{:S(2)}) %copy-start.4) | copy-done | bytes 1835032
  10.8 1.4 %copy-done.5 = bf16[1024,3,256]{2,0,1:T(8,128)(2,1)S(1)} copy-done((bf16[1024,3,256]{2,0,1:T(8,128)(2,1)S(1)}, bf16[1024,3,256]{2,0,1:T(8,128)(2,1)}, u32[]{:S(2)}) %copy-start.5) | copy-done | bytes 1572888
  12.2 1.0 copy-done.8
  13.3 43.1 %project.1 = (f32[256,1024]{1,0:T(8,128)S(1)}, bf16[8,4,128,256]{3,2,1,0:T(8,128)(2,1)S(1)}, bf16[8,2,64,256]{3,2,1,0:T(8,128)(2,1)S(1)}) custom-call(bf16[256,896]{1,0:T(8,128)(2,1)S(1)} %copy-done.8, bf16[896,1024]{1,0:T(8,128)(2,1)S(1)} %copy-done.4, bf16[80,256]{1,0:T(8,128)(2,1)S(1)} %fusion.3.mixed_ref, bf16[80,1024]{1,0:T(8,128)(2,1)S(1)} %copy-done.9, ...), custom_call_target="tpu_custom_call" | custom-call | tf_op jit(solution)/shard_map/project/pallas_call | solution.py:489
  56.3 1.3 copy-done.1
  57.7 0.8 copy-done.6
  58.5 0.0 all-gather.2.cloned.1.call-update
  58.5 0.1 tile.10
  58.6 0.1 broadcast_add_fusion
  58.7 0.1 add.94
  58.8 0.5 convert_reduce_fusion
  59.3 0.1 copy.16.ends_ref
  59.4 0.2 select_reduce_fusion
  59.6 1.6 %copy-done.2 = bf16[8,4,128,256]{3,2,1,0:T(8,128)(2,1)S(1)} copy-done((bf16[8,4,128,256]{3,2,1,0:T(8,128)(2,1)S(1)}, bf16[8,4,128,256]{3,2,1,0:T(8,128)(2,1)}, u32[]{:S(2)}) %copy-start.2) | copy-done | bytes 2097176
  61.2 1.0 copy-done.7
  62.2 42.7 %attend.1 = bf16[16,64,256]{2,1,0:T(8,128)(2,1)S(1)} custom-call(s32[16]{0:T(128)S(1)} %get-tuple-element.16.natural_ref, s32[16]{0:T(128)S(1)} %get-tuple-element.15.place_ref, s32[16]{0:T(128)S(1)} %multiply_add_fusion.first_ref, s32[128,1]{1,0:T(8,128)S(1)} %copy.16.ends_ref, bf16[16,64,256]{2,1,0:T(8,128)(2,1)S(1)} %bitcast.24, ...), custom_call_target="tpu_custom_call" | custom-call | tf_op jit(solution)/shard_map/attend/pallas_call | solution.py:344
  104.9 0.0 copy-start.3
  104.9 0.8 copy-done.3
  105.7 20.4 %give_back.1 = bf16[16,64,256]{2,1,0:T(8,128)(2,1)} custom-call(bf16[8,2,64,256]{3,2,1,0:T(8,128)(2,1)} %bitcast.22), custom_call_target="tpu_custom_call" | custom-call | tf_op jit(solution)/shard_map/give_back/pallas_call | solution.py:554
  126.2 0.0 all-gather.2.cloned.1.call-done
  126.2 0.0 copy-start.11
  126.2 2.6 %fusion.7 = (f32[256]{0:T(256)S(1)}, f32[256,1024]{1,0:T(8,128)S(1)}) fusion(f32[256,1024]{1,0:T(8,128)S(1)} %get-tuple-element.11, bf16[1024,256]{1,0:T(8,128)(2,1)} %bitcast.25, bf16[1024,1024]{1,0:T(8,128)(2,1)} %all-gather.2.cloned.1.call-done), kind=kOutput, calls=%fused_computation.33 | convolution fusion | flops 537394944 | bytes 4719616 | tf_op jit(solution)/shard_map/dot_general | solution.py:564
  128.8 0.3 multiply_reduce_fusion
  129.1 1.0 fusion
  (27 shorter events, 0.2 us)
Async XLA Ops:
  6.5 1.6 %copy-start = (f32[256,2048]{1,0:T(8,128)S(1)}, f32[256,2048]{1,0:T(8,128)}, u32[]{:S(2)}) copy-start(f32[256,2048]{1,0:T(8,128)} %param.20) | copy-start | bytes 6291460
  6.5 2.7 %copy-start.13 = (f32[256,80]{0,1:T(8,128)S(1)}, f32[256,80]{0,1:T(8,128)}, u32[]{:S(2)}) copy-start(f32[256,80]{0,1:T(8,128)} %param.17) | copy-start | bytes 245764
  6.5 2.7 %copy-start.12 = (f32[256,80]{0,1:T(8,128)S(1)}, f32[256,80]{0,1:T(8,128)}, u32[]{:S(2)}) copy-start(f32[256,80]{0,1:T(8,128)} %param.16) | copy-start | bytes 245764
  6.5 2.8 %copy-start.9 = (bf16[80,1024]{1,0:T(8,128)(2,1)S(1)}, bf16[80,1024]{1,0:T(8,128)(2,1)}, u32[]{:S(2)}) copy-start(bf16[80,1024]{1,0:T(8,128)(2,1)} %lift_ref.1) | copy-start | bytes 491524
  6.5 2.8 %copy-start.10 = (f32[4,1024]{1,0:T(4,128)S(1)}, f32[4,1024]{1,0:T(4,128)}, u32[]{:S(2)}) copy-start(f32[4,1024]{1,0:T(4,128)} %phase_ref.1) | copy-start | bytes 49156
  6.5 119.6 %all-gather.2.cloned.1.call-start = ((), (), s32[]{:S(2)}) async-start(), calls=%async_computation | async-start | bytes 2621440 | tf_op jit(solution)/shard_map/all_gather | solution.py:525
  9.3 1.5 %copy-start.4 = (bf16[896,1024]{1,0:T(8,128)(2,1)S(1)}, bf16[896,1024]{1,0:T(8,128)(2,1)}, u32[]{:S(2)}) copy-start(bf16[896,1024]{1,0:T(8,128)(2,1)} %proj_ref.1) | copy-start | bytes 5505028
  10.8 1.4 %copy-start.5 = (bf16[1024,3,256]{2,0,1:T(8,128)(2,1)S(1)}, bf16[1024,3,256]{2,0,1:T(8,128)(2,1)}, u32[]{:S(2)}) copy-start(bf16[1024,3,256]{2,0,1:T(8,128)(2,1)} %param.21) | copy-start | bytes 4718596
  12.2 1.0 copy-start.8
  13.3 45.5 %copy-start.14 = (s32[8192]{0:T(1024)S(1)}, s32[8192]{0:T(1024)}, u32[]{:S(2)}) copy-start(s32[8192]{0:T(1024)} %param.24) | copy-start | bytes 98308
  13.3 46.1 %copy-start.15 = (s32[16]{0:T(128)S(1)}, s32[16]{0:T(128)}, u32[]{:S(2)}) copy-start(s32[16]{0:T(128)} %param.25) | copy-start | bytes 196
  56.3 1.3 copy-start.1
  57.7 0.8 copy-start.6
  59.6 1.6 %copy-start.2 = (bf16[8,4,128,256]{3,2,1,0:T(8,128)(2,1)S(1)}, bf16[8,4,128,256]{3,2,1,0:T(8,128)(2,1)}, u32[]{:S(2)}) copy-start(bf16[8,4,128,256]{3,2,1,0:T(8,128)(2,1)} %copy-done.1) | copy-start | bytes 6291460
  61.2 1.0 copy-start.7
  104.9 0.8 copy-start.3
  126.2 2.9 %copy-start.11 = (bf16[1024,80]{0,1:T(8,128)(2,1)S(1)}, bf16[1024,80]{0,1:T(8,128)(2,1)}, u32[]{:S(2)}) copy-start(bf16[1024,80]{0,1:T(8,128)(2,1)} %param.23) | copy-start | bytes 491524
Sparse Core Ops, SparseCore 0:
  58.6 49.9 all-gather.1
